TPU v7x, 256 devices: a whole 4x4x8 slice. The times are simulated.
256 devices in a mesh: dp: 4 (over x), expert: 64 (over y, z, core).
Axes of the slice: x: 4, y: 4, z: 8, core: 2. Of those that a mesh axis runs over, the one named last changes fastest.
Arguments:
- tokens: bfloat16 [8192, 4096], P('expert', 'dp'), may hold values from -6 to 6
- expert_ids: int32 [8192, 2], P('expert'), may hold values from 0 to 63, all different within a row; in each aligned block of 128 rows (0 to 127, 128 to 255, ...) at most 5 rows name the same one
- route_weights: float32 [8192, 2], P('expert'), may hold values from 0.1 to 1
- w_gate: bfloat16 [14336, 4096], P('expert', 'dp'), may hold values from -0.09375 to 0.09375
- w_up: bfloat16 [14336, 4096], P('expert', 'dp'), may hold values from -0.09375 to 0.09375
- w_down: bfloat16 [14336, 4096], P('expert', 'dp'), may hold values from -0.125 to 0.125
- out_grad: bfloat16 [8192, 4096], P('expert', 'dp'), may hold values from -0.59765625 to 0.59765625
Outputs:
- output: bfloat16 [8192, 4096], P('expert', 'dp')
- grad_gate: bfloat16 [14336, 4096], P('expert', 'dp')
- grad_up: bfloat16 [14336, 4096], P('expert', 'dp')
- grad_down: bfloat16 [14336, 4096], P('expert', 'dp')
Inputs may be any that keep to these rules, and one draw needn't show every extreme that they name: `expert_ids`: each token names two different experts. Among the 128 tokens of one index of expert (aligned blocks of 128 rows), no expert is named more than 5 times, a bound that some block reaches.
All inputs are finite; a program needn't handle non-finite values.
Results may differ from a plain program's by a relative error of at most 0.029.
Values may be sent and summed in bfloat16 or wider, within the bound.
A program may use at most 128 MiB of HBM per device.

v0:
```python
import jax
import jax.numpy as jnp
from jax import lax
from jax.sharding import PartitionSpec as P


def from_partner(block, axis, bit):
    count = lax.axis_size(axis)
    route = []
    for low in range(count):
        high = low | 1 << bit
        if high != low and high < count:
            route += [(low, high), (high, low)]
    return lax.ppermute(block, axis, route)


def silu_parts(gate_sum):
    gate_sigmoid = jax.nn.sigmoid(gate_sum)
    return (gate_sum * gate_sigmoid, gate_sigmoid * (1.0 + gate_sum * (1.0 - gate_sigmoid)))


def relay_join(own_part, their_part, is_upper, join_axis):
    lower_first = jnp.concatenate([own_part, their_part], axis=join_axis)
    upper_first = jnp.concatenate([their_part, own_part], axis=join_axis)
    return jnp.where(is_upper, upper_first, lower_first)


def add_round(own_part, their_part):
    return (own_part.astype(jnp.float32) + their_part.astype(jnp.float32)).astype(jnp.bfloat16)


def forward_sums(in_rows, gate_w, up_w):
    contract_feats = (((1,), (1,)), ((), ()))
    part_gate = lax.dot_general(in_rows, gate_w, contract_feats, preferred_element_type=jnp.float32)
    part_up = lax.dot_general(in_rows, up_w, contract_feats, preferred_element_type=jnp.float32)
    gate_sum, up_sum = (
        lax.psum(part_gate.astype(jnp.bfloat16), "dp").astype(jnp.float32),
        lax.psum(part_up.astype(jnp.bfloat16), "dp").astype(jnp.float32),
    )
    active, slope_term = silu_parts(gate_sum)
    hidden = (active * up_sum).astype(jnp.bfloat16)
    return (up_sum, active, slope_term, hidden)


def backward_rows(cot_rows, down_w, up_sum, active, slope_term):
    contract_feats = (((1,), (1,)), ((), ()))
    part_hidden = lax.dot_general(
        cot_rows, down_w, contract_feats, preferred_element_type=jnp.float32
    )
    grad_hidden = lax.psum(part_hidden.astype(jnp.bfloat16), "dp").astype(jnp.float32)
    grad_gate_rows = (grad_hidden * up_sum * slope_term).astype(jnp.bfloat16)
    grad_up_rows = (grad_hidden * active).astype(jnp.bfloat16)
    return (grad_gate_rows, grad_up_rows)


def per_device(tokens, expert_ids, route_weights, w_gate, w_up, w_down, out_grad):
    experts = lax.axis_size("expert")
    copies = experts // 8
    levels = copies.bit_length() - 1
    owner_index = lax.axis_index("expert")
    copy_index = owner_index % copies
    tok_rows = tokens.shape[0]
    feat_cols = tokens.shape[1]
    shard_width = w_gate.shape[0]
    pair_count = 2 * tok_rows
    capacity = max(2, 5 * tok_rows // (2 * experts))
    buckets = experts * capacity
    flat_ids = expert_ids.reshape(pair_count)
    choose = (flat_ids[:, None] == jnp.arange(experts, dtype=jnp.int32)[None, :]).astype(jnp.int32)
    before = jnp.cumsum(choose, axis=0) - choose
    slot_index = jnp.sum(before * choose, axis=1)
    target = flat_ids * capacity + slot_index
    placer = (jnp.arange(buckets, dtype=jnp.int32)[:, None] == target[None, :]).astype(jnp.bfloat16)
    token_placer = jnp.sum(placer.reshape(buckets, tok_rows, 2), axis=2)
    send_rows = jnp.dot(token_placer, tokens, preferred_element_type=jnp.float32).astype(
        jnp.bfloat16
    )
    arrived = lax.all_to_all(
        send_rows.reshape(experts, capacity, feat_cols),
        "expert",
        split_axis=0,
        concat_axis=0,
        tiled=True,
    )
    in_rows = arrived.reshape(buckets, feat_cols)
    pieces = (w_gate, w_up, w_down)
    for bit_index in range(levels):
        partner = from_partner((pieces[0], pieces[1], pieces[2]), "expert", bit_index)
        is_upper = owner_index // 2**bit_index % 2 == 1
        pieces = (
            relay_join(pieces[0], partner[0], is_upper, 0),
            relay_join(pieces[1], partner[1], is_upper, 0),
            relay_join(pieces[2], partner[2], is_upper, 0),
        )
    gate_w, up_w, down_w = pieces
    up_sum, active, slope_term, hidden = forward_sums(in_rows, gate_w, up_w)
    out_rows = jnp.dot(hidden, down_w, preferred_element_type=jnp.float32).astype(jnp.bfloat16)
    returned = lax.all_to_all(
        out_rows.reshape(experts, capacity, feat_cols),
        "expert",
        split_axis=0,
        concat_axis=0,
        tiled=True,
    )
    picked = jnp.dot(
        placer.T, returned.reshape(buckets, feat_cols), preferred_element_type=jnp.float32
    )
    combined = jnp.sum(route_weights[:, :, None] * picked.reshape(tok_rows, 2, feat_cols), axis=1)
    output = combined.astype(jnp.bfloat16)
    cot_pairs = (route_weights[:, :, None] * out_grad[:, None, :].astype(jnp.float32)).astype(
        jnp.bfloat16
    )
    cot_send = jnp.dot(
        placer, cot_pairs.reshape(pair_count, feat_cols), preferred_element_type=jnp.float32
    ).astype(jnp.bfloat16)
    cot_arrived = lax.all_to_all(
        cot_send.reshape(experts, capacity, feat_cols),
        "expert",
        split_axis=0,
        concat_axis=0,
        tiled=True,
    )
    cot_rows = cot_arrived.reshape(buckets, feat_cols)
    contract_rows = (((0,), (0,)), ((), ()))
    grad_gate_rows, grad_up_rows = backward_rows(cot_rows, down_w, up_sum, active, slope_term)
    gate_term = lax.dot_general(
        grad_gate_rows, in_rows, contract_rows, preferred_element_type=jnp.float32
    ).astype(jnp.bfloat16)
    up_term = lax.dot_general(
        grad_up_rows, in_rows, contract_rows, preferred_element_type=jnp.float32
    ).astype(jnp.bfloat16)
    down_term = lax.dot_general(
        hidden, cot_rows, contract_rows, preferred_element_type=jnp.float32
    ).astype(jnp.bfloat16)
    grad_terms = (gate_term, up_term, down_term)
    for bit_index in range(levels):
        partner = from_partner((grad_terms[0], grad_terms[1], grad_terms[2]), "expert", bit_index)
        grad_terms = (
            add_round(grad_terms[0], partner[0]),
            add_round(grad_terms[1], partner[1]),
            add_round(grad_terms[2], partner[2]),
        )
    start_row = copy_index * shard_width
    grad_gate = lax.dynamic_slice_in_dim(grad_terms[0], start_row, shard_width, 0)
    grad_up = lax.dynamic_slice_in_dim(grad_terms[1], start_row, shard_width, 0)
    grad_down = lax.dynamic_slice_in_dim(grad_terms[2], start_row, shard_width, 0)
    return (output, grad_gate, grad_up, grad_down)


def solution(mesh):
    placed = (
        P("expert", "dp"),
        P("expert", None),
        P("expert", None),
        P("expert", "dp"),
        P("expert", "dp"),
        P("expert", "dp"),
        P("expert", "dp"),
    )
    return jax.shard_map(
        per_device,
        mesh=mesh,
        in_specs=placed,
        out_specs=(P("expert", "dp"), P("expert", "dp"), P("expert", "dp"), P("expert", "dp")),
        check_vma=False,
    )
```

profile of v0, /device:TPU:64, one launch (start us, length us, event | category | flops | bytes accessed | tf_op | source)
XLA Modules:
  0.0 1095.1 jit_solution(9500502577758955945)
XLA Ops:
  15.9 10.5 all-to-all-start
  26.7 2.8 maximum_select_fusion.12
  33.0 8.8 collective-permute-done.4
  41.8 3.6 maximum_select_fusion.10
  49.8 50.9 %all-to-all-done = bf16[64,5,1024]{2,1,0:T(8,128)(2,1)S(1)} async-done(((bf16[64,5,1024]{2,1,0:T(8,128)(2,1)}), bf16[64,5,1024]{2,1,0:T(8,128)(2,1)S(1)}, u32[]{:S(2)}, u32[]{:S(2)}) %all-to-all-start) | async-done | bytes 655392 | tf_op jit(solution)/shard_map/all_to_all | solution.py:78
  100.7 8.3 all-to-all-start.2
  109.3 8.5 collective-permute-done.1
  117.8 4.3 maximum_select_fusion.9
  123.4 14.9 %collective-permute-done.7 = bf16[448,1024]{1,0:T(8,128)(2,1)} collective-permute-done((bf16[448,1024]{1,0:T(8,128)(2,1)}, bf16[448,1024]{1,0:T(8,128)(2,1)}, u32[]{:S(2)}, u32[]{:S(2)}) %collective-permute-start.7) | collective-permute-done | bytes 917536 | tf_op jit(solution)/shard_map/ppermute | solution.py:14
  138.2 4.3 maximum_select_fusion.11
  144.8 15.9 %all-to-all-done.2 = bf16[64,5,1024]{2,1,0:T(8,128)(2,1)S(1)} async-done(((bf16[64,5,1024]{2,1,0:T(8,128)(2,1)}), bf16[64,5,1024]{2,1,0:T(8,128)(2,1)S(1)}, u32[]{:S(2)}, u32[]{:S(2)}) %all-to-all-start.2) | async-done | bytes 655392 | tf_op jit(solution)/shard_map/all_to_all | solution.py:116
  161.0 5.7 fusion.14
  166.7 109.0 %collective-permute-done.2 = bf16[896,1024]{1,0:T(8,128)(2,1)} collective-permute-done((bf16[896,1024]{1,0:T(8,128)(2,1)}, bf16[896,1024]{1,0:T(8,128)(2,1)}, u32[]{:S(2)}, u32[]{:S(2)}) %collective-permute-start.2) | collective-permute-done | bytes 1835040 | tf_op jit(solution)/shard_map/ppermute | solution.py:14
  275.6 5.6 fusion.15
  281.2 33.7 %collective-permute-done.8 = bf16[896,1024]{1,0:T(8,128)(2,1)} collective-permute-done((bf16[896,1024]{1,0:T(8,128)(2,1)}, bf16[896,1024]{1,0:T(8,128)(2,1)}, u32[]{:S(2)}, u32[]{:S(2)}) %collective-permute-start.8) | collective-permute-done | bytes 1835040 | tf_op jit(solution)/shard_map/ppermute | solution.py:14
  314.9 5.7 convolution_convert_fusion.3
  320.6 90.2 %all-reduce.3.cloned.1.call-done = (bf16[320,1792]{1,0:T(8,128)(2,1)}, bf16[320,1792]{1,0:T(8,128)(2,1)}, bf16[320,1792]{1,0:T(8,128)(2,1)}) async-done(((bf16[320,1792]{1,0:T(8,128)(2,1)}, bf16[320,1792]{1,0:T(8,128)(2,1)}, bf16[320,1792]{1,0:T(8,128)(2,1)}), (bf16[320,1792]{1,0:T(8,128)(2,1)}, bf16[320,1792]{1,0:T(8,128)(2,1)}, bf16[320,1792]{1,0:T(8,128)(2,1)})) %all-reduce.3.cloned.1.call-update) | async-done | bytes 3440656 | tf_op jit(solution)/shard_map/psum | solution.py:38
  410.8 4.8 convolution_convert_fusion.2
  416.0 2.3 convolution_convert_fusion.1
  418.8 2.3 convolution_convert_fusion
  436.3 70.1 %collective-permute-done.10 = bf16[1792,1024]{1,0:T(8,128)(2,1)S(1)} collective-permute-done((bf16[1792,1024]{1,0:T(8,128)(2,1)S(1)}, bf16[1792,1024]{1,0:T(8,128)(2,1)S(1)}, u32[]{:S(2)}, u32[]{:S(2)}) %collective-permute-start.10) | collective-permute-done | bytes 3670048 | tf_op jit(solution)/shard_map/ppermute | solution.py:14
  506.4 3.6 add_convert_fusion.4
  510.4 152.4 %collective-permute-done.13 = bf16[1792,1024]{1,0:T(8,128)(2,1)S(1)} collective-permute-done((bf16[1792,1024]{1,0:T(8,128)(2,1)S(1)}, bf16[1792,1024]{1,0:T(8,128)(2,1)S(1)}, u32[]{:S(2)}, u32[]{:S(2)}) %collective-permute-start.13) | collective-permute-done | bytes 3670048 | tf_op jit(solution)/shard_map/ppermute | solution.py:14
  662.8 3.7 add_convert_fusion.2
  667.8 72.9 %collective-permute-done.16 = bf16[1792,1024]{1,0:T(8,128)(2,1)S(1)} collective-permute-done((bf16[1792,1024]{1,0:T(8,128)(2,1)S(1)}, bf16[1792,1024]{1,0:T(8,128)(2,1)S(1)}, u32[]{:S(2)}, u32[]{:S(2)}) %collective-permute-start.16) | collective-permute-done | bytes 3670048 | tf_op jit(solution)/shard_map/ppermute | solution.py:14
  740.7 3.6 add_convert_fusion
  745.7 5.2 convolution_convert_fusion.6
  752.2 10.6 all-to-all-start.1
  763.1 317.0 %all-to-all-done.1 = bf16[64,5,1024]{2,1,0:T(8,128)(2,1)S(1)} async-done(((bf16[64,5,1024]{2,1,0:T(8,128)(2,1)}), bf16[64,5,1024]{2,1,0:T(8,128)(2,1)S(1)}, u32[]{:S(2)}, u32[]{:S(2)}) %all-to-all-start.1) | async-done | bytes 655392 | tf_op jit(solution)/shard_map/all_to_all | solution.py:98
  1081.6 2.1 add_convert_fusion.8
  1083.6 2.1 add_convert_fusion.7
  1085.7 2.1 add_convert_fusion.6
  (84 shorter events, 42.9 us)
Async XLA Ops:
  7.2 7.2 copy-start
  7.2 3.6 collective-permute-start.3
  7.3 19.4 %collective-permute-start = (bf16[224,1024]{1,0:T(8,128)(2,1)}, bf16[224,1024]{1,0:T(8,128)(2,1)}, u32[]{:S(2)}, u32[]{:S(2)}) collective-permute-start(bf16[224,1024]{1,0:T(8,128)(2,1)} %param.10), channel_id=1, source_target_pairs={{0,1},{1,0},{2,3},{3,2},{4,5},{5,4},{6,7},{7,6},{8,9},{9,8},{10,11... | collective-permute-start | bytes 1376264 | tf_op jit(solution)/shard_map/ppermute | solution.py:14
  12.3 29.5 %collective-permute-start.4 = (bf16[448,1024]{1,0:T(8,128)(2,1)S(1)}, bf16[448,1024]{1,0:T(8,128)(2,1)}, u32[]{:S(2)}, u32[]{:S(2)}) collective-permute-start(bf16[448,1024]{1,0:T(8,128)(2,1)S(1)} %maximum_select_fusion.13), channel_id=1, source_target_pairs={{0,2},{2,0},{1,3},{3,1},{4,6},{6,4},{5,7},{7,5},{8,10},{10,8},{9,1... | collective-permute-start | bytes 2752520 | tf_op jit(solution)/shard_map/ppermute | solution.py:14
  15.9 15.0 %copy-start.2 = (bf16[224,1024]{1,0:T(8,128)(2,1)S(1)}, bf16[224,1024]{1,0:T(8,128)(2,1)}, u32[]{:S(2)}) copy-start(bf16[224,1024]{1,0:T(8,128)(2,1)} %param.12) | copy-start | bytes 1376260
  15.9 84.8 %all-to-all-start = ((bf16[64,5,1024]{2,1,0:T(8,128)(2,1)}), bf16[64,5,1024]{2,1,0:T(8,128)(2,1)S(1)}, u32[]{:S(2)}, u32[]{:S(2)}) async-start(bf16[64,5,1024]{2,1,0:T(8,128)(2,1)} %reshape.98), calls=%async_computation | async-start | bytes 2097152 | tf_op jit(solution)/shard_map/all_to_all | solution.py:78
  26.5 4.5 collective-permute-start.6
  29.5 88.3 %collective-permute-start.1 = (bf16[448,1024]{1,0:T(8,128)(2,1)}, bf16[448,1024]{1,0:T(8,128)(2,1)}, u32[]{:S(2)}, u32[]{:S(2)}) collective-permute-start(bf16[448,1024]{1,0:T(8,128)(2,1)} %maximum_select_fusion.12), channel_id=1, source_target_pairs={{0,2},{2,0},{1,3},{3,1},{4,6},{6,4},{5,7},{7,5},{8,10},{10,8},{9,1... | collective-permute-start | bytes 2752520 | tf_op jit(solution)/shard_map/ppermute | solution.py:14
  32.4 14.5 %copy-start.3 = (bf16[128,1024]{1,0:T(8,128)(2,1)S(1)}, bf16[128,1024]{1,0:T(8,128)(2,1)}, u32[]{:S(2)}) copy-start(bf16[128,1024]{1,0:T(8,128)(2,1)} %param.13) | copy-start | bytes 786436
  32.4 105.8 %collective-permute-start.7 = (bf16[448,1024]{1,0:T(8,128)(2,1)}, bf16[448,1024]{1,0:T(8,128)(2,1)}, u32[]{:S(2)}, u32[]{:S(2)}) collective-permute-start(bf16[448,1024]{1,0:T(8,128)(2,1)} %maximum_select_fusion.14), channel_id=1, source_target_pairs={{0,2},{2,0},{1,3},{3,1},{4,6},{6,4},{5,7},{7,5},{8,10},{10,8},{9,1... | collective-permute-start | bytes 2752520 | tf_op jit(solution)/shard_map/ppermute | solution.py:14
  45.4 2.5 copy-start.4
  45.4 115.6 %collective-permute-start.5 = (bf16[896,1024]{1,0:T(8,128)(2,1)}, bf16[896,1024]{1,0:T(8,128)(2,1)}, u32[]{:S(2)}, u32[]{:S(2)}) collective-permute-start(bf16[896,1024]{1,0:T(8,128)(2,1)} %maximum_select_fusion.10), channel_id=1, source_target_pairs={{0,4},{4,0},{1,5},{5,1},{2,6},{6,2},{3,7},{7,3},{8,12},{12,8},{9,1... | collective-permute-start | bytes 5505032 | tf_op jit(solution)/shard_map/ppermute | solution.py:14
  100.7 59.9 %all-to-all-start.2 = ((bf16[64,5,1024]{2,1,0:T(8,128)(2,1)}), bf16[64,5,1024]{2,1,0:T(8,128)(2,1)S(1)}, u32[]{:S(2)}, u32[]{:S(2)}) async-start(bf16[64,5,1024]{2,1,0:T(8,128)(2,1)} %reshape.102), calls=%async_computation.2 | async-start | bytes 2097152 | tf_op jit(solution)/shard_map/all_to_all | solution.py:116
  109.1 301.7 %all-reduce.3.cloned.1.call-start = ((), (), s32[]{:S(2)}) async-start(), calls=%async_computation.3 | async-start | bytes 6881280 | tf_op jit(solution)/shard_map/psum | solution.py:38
  122.1 153.5 %collective-permute-start.2 = (bf16[896,1024]{1,0:T(8,128)(2,1)}, bf16[896,1024]{1,0:T(8,128)(2,1)}, u32[]{:S(2)}, u32[]{:S(2)}) collective-permute-start(bf16[896,1024]{1,0:T(8,128)(2,1)} %maximum_select_fusion.9), channel_id=1, source_target_pairs={{0,4},{4,0},{1,5},{5,1},{2,6},{6,2},{3,7},{7,3},{8,12},{12,8},{9,1... | collective-permute-start | bytes 5505032 | tf_op jit(solution)/shard_map/ppermute | solution.py:14
  142.6 172.3 %collective-permute-start.8 = (bf16[896,1024]{1,0:T(8,128)(2,1)}, bf16[896,1024]{1,0:T(8,128)(2,1)}, u32[]{:S(2)}, u32[]{:S(2)}) collective-permute-start(bf16[896,1024]{1,0:T(8,128)(2,1)} %maximum_select_fusion.11), channel_id=1, source_target_pairs={{0,4},{4,0},{1,5},{5,1},{2,6},{6,2},{3,7},{7,3},{8,12},{12,8},{9,1... | collective-permute-start | bytes 5505032 | tf_op jit(solution)/shard_map/ppermute | solution.py:14
  410.8 5.2 copy-start.7
  410.8 5.2 copy-start.9
  415.6 3.2 copy-start.5
  415.6 6.7 collective-permute-start.9
  418.2 9.3 collective-permute-start.12
  421.1 11.7 %collective-permute-start.15 = (bf16[1792,1024]{1,0:T(8,128)(2,1)S(1)}, bf16[1792,1024]{1,0:T(8,128)(2,1)S(1)}, u32[]{:S(2)}, u32[]{:S(2)}) collective-permute-start(bf16[1792,1024]{1,0:T(8,128)(2,1)S(1)} %convolution_convert_fusion), channel_id=1, source_target_pairs={{0,1},{1,0},{2,3},{3,2},{4,5},{5,4},{6,7},{7,6},{8,9},{9,8},{10,11... | collective-permute-start | bytes 11010056 | tf_op jit(solution)/shard_map/ppermute | solution.py:14
  424.2 82.3 %collective-permute-start.10 = (bf16[1792,1024]{1,0:T(8,128)(2,1)S(1)}, bf16[1792,1024]{1,0:T(8,128)(2,1)S(1)}, u32[]{:S(2)}, u32[]{:S(2)}) collective-permute-start(bf16[1792,1024]{1,0:T(8,128)(2,1)S(1)} %add_convert_fusion.5), channel_id=1, source_target_pairs={{0,2},{2,0},{1,3},{3,1},{4,6},{6,4},{5,7},{7,5},{8,10},{10,8},{9,1... | collective-permute-start | bytes 11010056 | tf_op jit(solution)/shard_map/ppermute | solution.py:14
  429.4 233.4 %collective-permute-start.13 = (bf16[1792,1024]{1,0:T(8,128)(2,1)S(1)}, bf16[1792,1024]{1,0:T(8,128)(2,1)S(1)}, u32[]{:S(2)}, u32[]{:S(2)}) collective-permute-start(bf16[1792,1024]{1,0:T(8,128)(2,1)S(1)} %add_convert_fusion.3), channel_id=1, source_target_pairs={{0,2},{2,0},{1,3},{3,1},{4,6},{6,4},{5,7},{7,5},{8,10},{10,8},{9,1... | collective-permute-start | bytes 11010056 | tf_op jit(solution)/shard_map/ppermute | solution.py:14
  434.7 306.1 %collective-permute-start.16 = (bf16[1792,1024]{1,0:T(8,128)(2,1)S(1)}, bf16[1792,1024]{1,0:T(8,128)(2,1)S(1)}, u32[]{:S(2)}, u32[]{:S(2)}) collective-permute-start(bf16[1792,1024]{1,0:T(8,128)(2,1)S(1)} %add_convert_fusion.1), channel_id=1, source_target_pairs={{0,2},{2,0},{1,3},{3,1},{4,6},{6,4},{5,7},{7,5},{8,10},{10,8},{9,1... | collective-permute-start | bytes 11010056 | tf_op jit(solution)/shard_map/ppermute | solution.py:14
  510.0 571.5 %collective-permute-start.11 = (bf16[1792,1024]{1,0:T(8,128)(2,1)}, bf16[1792,1024]{1,0:T(8,128)(2,1)}, u32[]{:S(2)}, u32[]{:S(2)}) collective-permute-start(bf16[1792,1024]{1,0:T(8,128)(2,1)} %add_convert_fusion.4), channel_id=1, source_target_pairs={{0,4},{4,0},{1,5},{5,1},{2,6},{6,2},{3,7},{7,3},{8,12},{12,8},{9,1... | collective-permute-start | bytes 11010056 | tf_op jit(solution)/shard_map/ppermute | solution.py:14
  666.5 79.2 %copy-start.6 = (bf16[320,1792]{1,0:T(8,128)(2,1)S(1)}, bf16[320,1792]{1,0:T(8,128)(2,1)}, u32[]{:S(2)}) copy-start(bf16[320,1792]{1,0:T(8,128)(2,1)} %get-tuple-element.4) | copy-start | bytes 3440644
  666.5 79.2 %copy-start.8 = (bf16[320,1792]{1,0:T(8,128)(2,1)S(1)}, bf16[320,1792]{1,0:T(8,128)(2,1)}, u32[]{:S(2)}) copy-start(bf16[320,1792]{1,0:T(8,128)(2,1)} %get-tuple-element.5) | copy-start | bytes 3440644
  666.5 417.1 %collective-permute-start.14 = (bf16[1792,1024]{1,0:T(8,128)(2,1)}, bf16[1792,1024]{1,0:T(8,128)(2,1)}, u32[]{:S(2)}, u32[]{:S(2)}) collective-permute-start(bf16[1792,1024]{1,0:T(8,128)(2,1)} %add_convert_fusion.2), channel_id=1, source_target_pairs={{0,4},{4,0},{1,5},{5,1},{2,6},{6,2},{3,7},{7,3},{8,12},{12,8},{9,1... | collective-permute-start | bytes 11010056 | tf_op jit(solution)/shard_map/ppermute | solution.py:14
  744.4 341.4 %collective-permute-start.17 = (bf16[1792,1024]{1,0:T(8,128)(2,1)}, bf16[1792,1024]{1,0:T(8,128)(2,1)}, u32[]{:S(2)}, u32[]{:S(2)}) collective-permute-start(bf16[1792,1024]{1,0:T(8,128)(2,1)} %add_convert_fusion), channel_id=1, source_target_pairs={{0,4},{4,0},{1,5},{5,1},{2,6},{6,2},{3,7},{7,3},{8,12},{12,8},{9,1... | collective-permute-start | bytes 11010056 | tf_op jit(solution)/shard_map/ppermute | solution.py:14
  752.2 327.9 %all-to-all-start.1 = ((bf16[64,5,1024]{2,1,0:T(8,128)(2,1)}), bf16[64,5,1024]{2,1,0:T(8,128)(2,1)S(1)}, u32[]{:S(2)}, u32[]{:S(2)}) async-start(bf16[64,5,1024]{2,1,0:T(8,128)(2,1)} %reshape.100), calls=%async_computation.1 | async-start | bytes 2097152 | tf_op jit(solution)/shard_map/all_to_all | solution.py:98
  1080.4 7.5 copy-start.1
Sparse Core Ops, SparseCore 0:
  320.7 89.9 all-reduce.2
where the time goes:
time: 1110 us; the launch traced here: 1100 us
  waiting for transfers between devices  949 us (85%)
  starting transfers between devices  48.4 us (4%)
  other arithmetic  42.3 us (4%)
  matrix products  33.5 us (3%)
  between operations  14.8 us (1%)
    ppermute x18, waiting for transfers between devices, from_partner(): return lax.ppermute(block, axis, route)  475 us
    all_to_all x1, waiting for transfers between devices, per_device(): lax.all_to_all(out_rows.reshape(experts, capacity, feat_cols), 'expert',...  317 us
    psum x1, waiting for transfers between devices, forward_sums(): lax.psum(part_up.astype(jnp.bfloat16), 'dp').astype(jnp.float32)  90.2 us
    all_to_all x1, waiting for transfers between devices, per_device(): lax.all_to_all(send_rows.reshape(experts, capacity, feat_cols), 'expert',...  50.9 us
    convert_element_type x9, other arithmetic, add_round(): (own_part.astype(jnp.float32) + their_part.astype(jnp.float32)).astype(jn...  22.8 us
  transfers between devices with their start and end apart: 22, of which 15 were waited for; matrix products, arithmetic and copies ran while one was open for 6% of the time, Pallas kernels for 0%

commit v1 on v0

v1 whole, which is shorter than its diff:
```python
import jax
import jax.numpy as jnp
from jax import lax
from jax.experimental import pallas as pl
from jax.experimental.pallas import tpu as pltpu
from jax.sharding import PartitionSpec as P

NX, NY, NZ = 4, 4, 8
SLICES = 8
SLOT = 40
CODE = 64
TOK = 128
PER_Y = NZ * SLOT
ROWS = NY * PER_Y
CHUNK = 256
NCH = ROWS // CHUNK
WINDOW = 48
PIECES = ((0, 32, 0, 1), (32, 80, 0, 3), (112, 80, 2, 3), (192, 80, 4, 3), (272, 48, 6, 2))
PLACE = (0, 1, 3, 5, 7, 6, 4, 2)
MESH = pl.DeviceIdType.MESH
BF = jnp.bfloat16
F32 = jnp.float32
CROSS_LAST = (((1,), (1,)), ((), ()))
CROSS_FIRST = (((0,), (0,)), ((), ()))
PLAIN = (((1,), (0,)), ((), ()))


def dot(a, b, dims):
    return lax.dot_general(a, b, dims, preferred_element_type=F32)


def layer_kernel(
    tok_in, og_in, meta_in, wg, wu, wd,
    out, g_gate, g_up, g_down,
    w, meta, tb, gb, tx, cx, ts, cs,
    part, part_in, hid, part_h, part_h_in, grads_x,
    up_s, act_s, slope_s, rows_out, rows_back,
    ring_out, ring_in, acc, pair_out, pair_in,
    w_loc, w_send, w_recv, m_send, m_recv, own_sem,
    tz_send, tz_recv, gz_send, gz_recv, ty_send, ty_recv, cy_send, cy_recv,
    p_send, p_recv, h_send, h_recv, ph_send, ph_recv, gx_send, gx_recv,
    o_send, o_recv, r_send, r_recv, pair_send, pair_recv,
):
    own_h, feats = wg.shape
    half_f = feats // 2
    chip_h = 2 * own_h
    quarter_h = chip_h // NX
    x = lax.axis_index("dp")
    e = lax.axis_index("expert")
    c = lax.rem(e, 2)
    chip = e // 2
    z = lax.rem(chip, NZ)
    y = chip // NZ
    half = z // 4
    sibling = e + 1 - 2 * c

    def chip_at(dy, dz):
        return (x, (lax.rem(y + dy, NY) * NZ + lax.rem(z + dz, NZ)) * 2 + c)

    def x_peer(k):
        return lax.rem(x + k, NX)

    def remote(src, dst, send_sem, recv_sem, dev):
        return pltpu.make_async_remote_copy(
            src_ref=src, dst_ref=dst, send_sem=send_sem, recv_sem=recv_sem,
            device_id=dev, device_id_type=MESH)

    def wait_bytes(ref, sem):
        pltpu.make_async_copy(ref, ref, sem).wait()

    barrier = pltpu.get_barrier_semaphore()
    friends = [chip_at(0, d) for d in range(1, NZ)] + [chip_at(d, 0) for d in range(1, NY)]
    friends += [(x_peer(k), e) for k in range(1, NX)] + [(x, sibling)]
    for dev in friends:
        pl.semaphore_signal(barrier, inc=1, device_id=dev, device_id_type=MESH)
    pl.semaphore_wait(barrier, len(friends))

    def ring_send(own, buf, send, recv, k):
        for d in range(2):
            if k == 1:
                src, dst = own, buf.at[1 + d]
            else:
                src, dst = buf.at[2 * k - 3 + d], buf.at[2 * k - 1 + d if k < 4 else 7]
            if k == 4:
                lanes = pl.ds(d * half_f, half_f)
                src, dst = src.at[:, lanes], dst.at[:, lanes]
            remote(src, dst, send.at[d, k - 1], recv.at[d, k - 1], chip_at(0, 1 if d == 0 else NZ - 1)).start()

    def ring_wait(buf, recv, k):
        for d in range(2):
            ref = buf.at[1 + d] if k < 4 else buf.at[7, :, pl.ds(d * half_f, half_f)]
            wait_bytes(ref, recv.at[d, k - 1])

    pltpu.make_async_copy(tok_in, tb.at[0], own_sem.at[0]).start()
    for d in range(1, NZ):
        remote(meta_in, meta.at[PLACE[d]], m_send, m_recv, chip_at(0, d)).start()
    pltpu.make_async_copy(meta_in, meta.at[0], own_sem.at[2]).start()
    ring_send(tok_in, tb, tz_send, tz_recv, 1)
    pltpu.make_async_copy(og_in, gb.at[0], own_sem.at[1]).start()

    def w_part(i, core):
        return w.at[i, pl.ds(pl.multiple_of(core * own_h, 16), own_h)]

    for i, src in enumerate((wg, wu, wd)):
        remote(src, w_part(i, c), w_send.at[i], w_recv.at[i], (x, sibling)).start()
        pltpu.make_async_copy(src, w_part(i, c), w_loc.at[i]).start()

    wait_bytes(meta.at[0], own_sem.at[2])
    wait_bytes(meta.at[pl.ds(1, NZ - 1)], m_recv)

    def hits(dy, place, first, count):
        codes = meta[place, 0:2, :] - ((lax.rem(y + dy, NY) * 2 + half) * CODE).astype(F32)
        at = jnp.where((codes >= 0.0) & (codes < float(SLOT)), codes + float(place * SLOT), -1.0)
        row = (lax.broadcasted_iota(jnp.int32, (count, TOK), 0) + first).astype(F32)
        return row == at[0:1], row == at[1:2]

    def weights(dy, place, first, count):
        hit0, hit1 = hits(dy, place, first, count)
        return (jnp.where(hit0, meta[place, 2:3, :], 0.0) + jnp.where(hit1, meta[place, 3:4, :], 0.0))

    def select(p, buf, near, staged, send, recv, scaled):
        first, count, place, places = PIECES[p]
        wts = [[weights(dy, place + n, first, count) for n in range(places)] for dy in range(NY)]
        wts = jnp.concatenate([jnp.concatenate(r, axis=1) for r in wts], axis=0)
        picked = dot((wts > 0.0).astype(BF), buf[place:place + places].reshape(places * TOK, feats), PLAIN)
        if scaled:
            picked = jnp.sum(wts, axis=1, keepdims=True) * picked
        picked = picked.astype(BF)
        near[first:first + count] = picked[0:count]
        for dy in (1, 3, 2):
            staged[dy - 1, first:first + count] = picked[dy * count:(dy + 1) * count]
            remote(staged.at[dy - 1, pl.ds(first, count)],
                   near.at[pl.ds(dy * PER_Y + first, count)],
                   send.at[dy - 1], recv.at[dy - 1], chip_at(dy, 0)).start()

    def relay_step(k, own, buf, zs, zr, near, staged, ys, yr, scaled):
        ring_wait(buf, zr, k)
        if k < 4:
            ring_send(own, buf, zs, zr, k + 1)
        select(k, buf, near, staged, ys, yr, scaled)

    tok_args = (tok_in, tb, tz_send, tz_recv, tx, ts, ty_send, ty_recv, False)
    cot_args = (og_in, gb, gz_send, gz_recv, cx, cs, cy_send, cy_recv, True)
    wait_bytes(tb.at[0], own_sem.at[0])
    select(0, tb, tx, ts, ty_send, ty_recv, False)
    for k in range(1, 4):
        relay_step(k, *tok_args)
    ring_send(og_in, gb, gz_send, gz_recv, 1)
    relay_step(4, *tok_args)
    wait_bytes(gb.at[0], own_sem.at[1])
    select(0, gb, cx, cs, cy_send, cy_recv, True)

    def to_peers(src_of, dst, send, recv):
        for k in range(1, NX):
            x2 = x_peer(k)
            remote(src_of(x2), dst, send, recv, (x2, e)).start()

    def chunk(ref, i):
        start = i * CHUNK
        if not isinstance(i, int):
            start = pl.multiple_of(start, CHUNK)
        return ref[pl.ds(start, CHUNK)]

    def up_gate(i):
        rows = chunk(tx, i)
        for kind in range(2):
            prod = dot(w[kind], rows, CROSS_LAST).astype(BF)
            for q in range(NX):
                part[q, i, kind] = prod[q * quarter_h:(q + 1) * quarter_h]
        to_peers(lambda x2: part.at[x2, i], part_in.at[x, i], p_send.at[i], p_recv.at[i])

    def act(i):
        wait_bytes(part_in.at[pl.ds(0, NX - 1), i], p_recv.at[i])
        gate = part[x, i, 0].astype(F32)
        up = part[x, i, 1].astype(F32)
        for k in range(1, NX):
            gate += part_in[x_peer(k), i, 0].astype(F32)
            up += part_in[x_peer(k), i, 1].astype(F32)
        sig = jax.nn.sigmoid(gate)
        active = gate * sig
        up_s[i] = up
        act_s[i] = active
        slope_s[i] = sig * (1.0 + gate * (1.0 - sig))
        hid[i, x] = (active * up).astype(BF)
        to_peers(lambda x2: hid.at[i, x], hid.at[i, x], h_send.at[i], h_recv.at[i])

    def expert_out(i):
        wait_bytes(hid.at[i, pl.ds(0, NX - 1)], h_recv.at[i])
        rows_out[pl.ds(pl.multiple_of(i * CHUNK, CHUNK), CHUNK)] = dot(
            hid[i].reshape(chip_h, CHUNK), w[2], CROSS_FIRST).astype(BF)

    def hidden_part(i):
        prod = dot(w[2], chunk(cx, i), CROSS_LAST).astype(BF)
        for q in range(NX):
            part_h[q, i] = prod[q * quarter_h:(q + 1) * quarter_h]
        to_peers(lambda x2: part_h.at[x2, i], part_h_in.at[x, i], ph_send.at[i], ph_recv.at[i])

    def grad_rows(i):
        wait_bytes(part_h_in.at[pl.ds(0, NX - 1), i], ph_recv.at[i])
        gh = part_h[x, i].astype(F32)
        for k in range(1, NX):
            gh += part_h_in[x_peer(k), i].astype(F32)
        grads_x[i, x, 0] = (gh * up_s[i] * slope_s[i]).astype(BF)
        grads_x[i, x, 1] = (gh * act_s[i]).astype(BF)
        to_peers(lambda x2: grads_x.at[i, x], grads_x.at[i, x], gx_send.at[i], gx_recv.at[i])

    def down_step(i):
        acc[2] += dot(hid[i].reshape(chip_h, CHUNK), chunk(cx, i), PLAIN)

    def gate_step(i):
        wait_bytes(grads_x.at[i, pl.ds(0, NX - 1)], gx_recv.at[i])
        for kind in range(2):
            acc[kind] += dot(grads_x[i, :, kind].reshape(chip_h, CHUNK), chunk(tx, i), PLAIN)

    def loop(lo, hi, f):
        lax.fori_loop(lo, hi, lambda i, carry: (f(i), carry)[1], 0)

    def wait_rows(ref, recv, dy):
        wait_bytes(ref.at[pl.ds(dy * PER_Y, PER_Y)], recv.at[dy - 1])

    relay_step(1, *cot_args)
    for i, src in enumerate((wg, wu, wd)):
        wait_bytes(w_part(i, c), w_loc.at[i])
        wait_bytes(w_part(i, 1 - c), w_recv.at[i])
    up_gate(0)
    relay_step(2, *cot_args)
    wait_rows(tx, ty_recv, 1)
    wait_rows(tx, ty_recv, 3)
    wait_rows(tx, ty_recv, 2)
    loop(1, NCH, up_gate)
    relay_step(3, *cot_args)
    relay_step(4, *cot_args)
    loop(0, NCH, act)
    loop(0, NCH, expert_out)

    def give_back(p):
        first, count = PIECES[p][:2]
        for dy in (1, 3, 2):
            remote(rows_out.at[pl.ds(dy * PER_Y + first, count)],
                   rows_back.at[dy - 1, pl.ds(first, count)],
                   o_send.at[p], o_recv.at[p], chip_at(NY - dy, 0)).start()

    for p in (4, 3, 2, 1, 0):
        give_back(p)

    def await_piece(p):
        first, count = PIECES[p][:2]
        wait_bytes(rows_back.at[:, pl.ds(first, count)], o_recv.at[p])

    def dense(place):
        first = place * SLOT // 16 * 16
        rows = [rows_out[first:first + WINDOW]]
        rows += [rows_back[dy - 1, first:first + WINDOW] for dy in range(1, NY)]
        rows = jnp.concatenate(rows, axis=0)
        wts = jnp.concatenate([weights(dy, place, first, WINDOW) for dy in range(NY)], axis=0)
        coarse = wts.astype(BF)
        fine = (wts - coarse.astype(F32)).astype(BF)
        return dot(coarse, rows, CROSS_FIRST) + dot(fine, rows, CROSS_FIRST)

    def fold_send(k, d):
        src, dst = ring_out.at[d, k - 1], ring_in.at[d, k - 1]
        if k == 1:
            lanes = pl.ds(d * half_f, half_f)
            src, dst = src.at[:, lanes], dst.at[:, lanes]
        remote(src, dst, r_send.at[d, k - 1], r_recv.at[d, k - 1], chip_at(0, 1 if d == 0 else NZ - 1)).start()

    def fold_first():
        block = dense(7).astype(BF)
        for d in range(2):
            ring_out[d, 0] = block
            fold_send(1, d)

    def fold_wait(k, d):
        ref = ring_in.at[d, k - 1]
        wait_bytes(ref.at[:, pl.ds(d * half_f, half_f)] if k == 1 else ref, r_recv.at[d, k - 1])

    def fold(k):
        for d in range(2):
            block = dense(10 - 2 * k - d)
            fold_wait(k - 1, d)
            if k == 2:
                lanes = slice(d * half_f, (d + 1) * half_f)
                others = slice((1 - d) * half_f, (2 - d) * half_f)
                ring_out[d, 1, :, lanes] = (block[:, lanes] + ring_in[d, 0, :, lanes].astype(F32)).astype(BF)
                ring_out[d, 1, :, others] = block[:, others].astype(BF)
            else:
                ring_out[d, k - 1] = (block + ring_in[d, k - 2].astype(F32)).astype(BF)
            fold_send(k, d)

    for dy in (1, 3, 2):
        wait_rows(cx, cy_recv, dy)
    loop(0, NCH, hidden_part)
    acc[...] = jnp.zeros_like(acc)
    loop(0, NCH, grad_rows)
    await_piece(4)
    fold_first()
    loop(0, NCH, down_step)

    def send_pair(kind):
        pair_out[kind] = acc[kind, pl.ds(pl.multiple_of((1 - c) * own_h, 16), own_h)].astype(BF)
        remote(pair_out.at[kind], pair_in.at[kind], pair_send.at[kind], pair_recv.at[kind],
               (x, sibling)).start()

    send_pair(2)
    await_piece(3)
    fold(2)
    loop(0, 2, gate_step)
    await_piece(2)
    fold(3)
    loop(2, 4, gate_step)
    await_piece(1)
    fold(4)
    loop(4, NCH, gate_step)
    send_pair(0)
    send_pair(1)
    await_piece(0)
    mine = dense(0)

    def join_pair(kind, dest):
        wait_bytes(pair_in.at[kind], pair_recv.at[kind])
        dest[...] = (acc[kind, pl.ds(pl.multiple_of(c * own_h, 16), own_h)]
                     + pair_in[kind].astype(F32)).astype(BF)

    join_pair(2, g_down)
    join_pair(0, g_gate)
    join_pair(1, g_up)
    for d in range(2):
        fold_wait(4, d)
        mine += ring_in[d, 3].astype(F32)
    out[...] = mine.astype(BF)

    for i in range(3):
        wait_bytes(wg, w_send.at[i])
        wait_bytes(pair_out.at[i], pair_send.at[i])
    wait_bytes(meta.at[pl.ds(1, NZ - 1)], m_send)
    for d in range(2):
        lanes = pl.ds(d * half_f, half_f)
        for k in range(1, 5):
            for buf, sem in ((tb, tz_send), (gb, gz_send)):
                wait_bytes(buf.at[0] if k < 4 else buf.at[0, :, lanes], sem.at[d, k - 1])
            wait_bytes(ring_out.at[d, k - 1] if k > 1 else ring_out.at[d, 0, :, lanes], r_send.at[d, k - 1])
    for dy in range(1, NY):
        wait_bytes(ts.at[dy - 1], ty_send.at[dy - 1])
        wait_bytes(cs.at[dy - 1], cy_send.at[dy - 1])
    for p in range(5):
        wait_bytes(rows_back.at[:, pl.ds(0, PIECES[p][1])], o_send.at[p])
    for i in range(NCH):
        wait_bytes(part.at[pl.ds(0, NX - 1), i], p_send.at[i])
        wait_bytes(hid.at[i, pl.ds(0, NX - 1)], h_send.at[i])
        wait_bytes(part_h.at[pl.ds(0, NX - 1), i], ph_send.at[i])
        wait_bytes(grads_x.at[i, pl.ds(0, NX - 1)], gx_send.at[i])


def run_layer(tokens, out_grad, meta, wg, wu, wd):
    own_h, feats = wg.shape
    qh = 2 * own_h // NX
    dma = pltpu.SemaphoreType.DMA
    vm = pltpu.VMEM
    scratch = [
        vm((3, 2 * own_h, feats), BF), vm((NZ, 8, TOK), F32),
        vm((NZ, TOK, feats), BF), vm((NZ, TOK, feats), BF),
        vm((ROWS, feats), BF), vm((ROWS, feats), BF),
        vm((NY - 1, PER_Y, feats), BF), vm((NY - 1, PER_Y, feats), BF),
        vm((NX, NCH, 2, qh, CHUNK), BF), vm((NX, NCH, 2, qh, CHUNK), BF),
        vm((NCH, NX, qh, CHUNK), BF),
        vm((NX, NCH, qh, CHUNK), BF), vm((NX, NCH, qh, CHUNK), BF),
        vm((NCH, NX, 2, qh, CHUNK), BF),
        vm((NCH, qh, CHUNK), F32), vm((NCH, qh, CHUNK), F32), vm((NCH, qh, CHUNK), F32),
        vm((ROWS, feats), BF), vm((NY - 1, PER_Y, feats), BF),
        vm((2, 4, TOK, feats), BF), vm((2, 4, TOK, feats), BF),
        vm((3, 2 * own_h, feats), F32),
        vm((3, own_h, feats), BF), vm((3, own_h, feats), BF),
        dma((3,)), dma((3,)), dma((3,)), dma, dma, dma((3,)),
        dma((2, 4)), dma((2, 4)), dma((2, 4)), dma((2, 4)),
        dma((NY - 1,)), dma((NY - 1,)), dma((NY - 1,)), dma((NY - 1,)),
        dma((NCH,)), dma((NCH,)), dma((NCH,)), dma((NCH,)),
        dma((NCH,)), dma((NCH,)), dma((NCH,)), dma((NCH,)),
        dma((5,)), dma((5,)), dma((2, 4)), dma((2, 4)),
        dma((3,)), dma((3,)),
    ]
    anywhere = pl.BlockSpec(memory_space=pl.ANY)
    inside = pl.BlockSpec(memory_space=pltpu.VMEM)
    return pl.pallas_call(
        layer_kernel,
        out_shape=(
            jax.ShapeDtypeStruct((TOK, feats), BF),
            jax.ShapeDtypeStruct((own_h, feats), BF),
            jax.ShapeDtypeStruct((own_h, feats), BF),
            jax.ShapeDtypeStruct((own_h, feats), BF),
        ),
        in_specs=[anywhere] * 6,
        out_specs=[inside] * 4,
        scratch_shapes=scratch,
        compiler_params=pltpu.CompilerParams(
            collective_id=0, has_side_effects=True, vmem_limit_bytes=60 * 1024 * 1024),
    )(tokens, out_grad, meta, wg, wu, wd)


def per_device(tokens, expert_ids, route_weights, w_gate, w_up, w_down, out_grad):
    tok_rows = tokens.shape[0]
    slices = expert_ids // 8
    flat = slices.reshape(2 * tok_rows)
    choose = (flat[:, None] == jnp.arange(SLICES, dtype=jnp.int32)[None, :]).astype(jnp.int32)
    before = jnp.cumsum(choose, axis=0) - choose
    slot = jnp.sum(before * choose, axis=1).reshape(tok_rows, 2)
    code = (slices * CODE + slot).astype(F32)
    meta = jnp.concatenate([code.T, route_weights.T, jnp.zeros((4, tok_rows), F32)], axis=0)
    return run_layer(tokens, out_grad, meta, w_gate, w_up, w_down)


def solution(mesh):
    placed = (
        P("expert", "dp"),
        P("expert", None),
        P("expert", None),
        P("expert", "dp"),
        P("expert", "dp"),
        P("expert", "dp"),
        P("expert", "dp"),
    )
    return jax.shard_map(
        per_device,
        mesh=mesh,
        in_specs=placed,
        out_specs=(P("expert", "dp"), P("expert", "dp"), P("expert", "dp"), P("expert", "dp")),
        check_vma=False,
    )
```

time: 1110 us -> 133 us (0.12); the launches traced: 1100 us -> 131 us
  waiting for transfers between devices: 949 us -> 0 us
  Pallas kernels: 0 us -> 122 us
  starting transfers between devices: 48.4 us -> 0 us
  other arithmetic: 42.3 us -> 1.42 us
  matrix products: 33.5 us -> 0 us
  between operations: 14.8 us -> 0.7 us
    ppermute x18 -> x0, waiting for transfers between devices: 475 us -> none  [from_partner(): return lax.ppermute(block, axis, route)]
    all_to_all x3 -> x0, waiting for transfers between devices: 384 us -> none  [the longest x1 317 us: per_device(): lax.all_to_all(out_rows.reshape(experts, capacity, feat_cols), 'expert',...]
    pallas_call x0 -> x1, Pallas kernels: none -> 122 us  [run_layer(): pl.pallas_call(layer_kernel, out_shape=(jax.ShapeDtypeStruct((TOK, feats)...]
    psum x1 -> x0, waiting for transfers between devices: 90.2 us -> none  [forward_sums(): lax.psum(part_up.astype(jnp.bfloat16), 'dp').astype(jnp.float32)]
    dot_general x10 -> x0, matrix products: 33.5 us -> none  [the longest x1 5.7 us: forward_sums(): lax.dot_general(in_rows, up_w, contract_feats, preferred_element_type=jnp...]
    all_to_all x3 -> x0, starting transfers between devices: 29.5 us -> none  [the longest x1 10.6 us: per_device(): lax.all_to_all(out_rows.reshape(experts, capacity, feat_cols), 'expert',...]
    convert_element_type x10 -> x1, other arithmetic: 22.8 us -> 0.01 us  [per_device(): (flat[:, None] == jnp.arange(SLICES, dtype=jnp.int32)[None, :]).astype(jn...]
    ppermute x18 -> x0, starting transfers between devices: 18.7 us -> none  [from_partner(): return lax.ppermute(block, axis, route)]
  transfers between devices with their start and end apart: 22 -> 0, of which waited for: 15 -> 0; matrix products, arithmetic and copies ran while one was open for 6% -> 0% of each run, Pallas kernels for 0% -> 0%
where the time goes in v1:
time: 133 us; the launch traced here: 131 us
  Pallas kernels  122 us (92%)
  local copies, waits for them, and re-layouts  7.01 us (5%)
  other arithmetic  1.42 us (1%)
    pallas_call x1, Pallas kernels, run_layer(): pl.pallas_call(layer_kernel, out_shape=(jax.ShapeDtypeStruct((TOK, feats)...  122 us
    unnamed x14, local copies, waits for them, and re-layouts  6.13 us

profile of v1, /device:TPU:64, one launch (start us, length us, event | category | flops | bytes accessed | tf_op | source)
XLA Modules:
  0.0 131.3 jit_solution(10908831551745937679)
XLA Ops:
  0.6 0.0 copy-start.3
  0.7 0.1 pad.2.clone
  0.7 0.6 copy-done.3
  1.3 0.1 copy.11
  1.4 0.1 eq.29
  1.6 0.1 eq.25
  1.7 0.6 reduce-window.6
  2.3 0.2 slice_reduce_fusion
  2.6 0.1 fusion.1
  2.7 0.1 reshape.29
  2.8 0.1 copy.13
  2.9 0.0 copy-start.4
  2.9 0.7 copy-done.4
  3.6 0.7 maximum_maximum_fusion.meta_in
  4.3 122.2 %shard_map.102 = (bf16[128,1024]{1,0:T(8,128)(2,1)}, bf16[224,1024]{1,0:T(8,128)(2,1)}, bf16[224,1024]{1,0:T(8,128)(2,1)}, bf16[224,1024]{1,0:T(8,128)(2,1)}) custom-call(bf16[128,1024]{1,0:T(8,128)(2,1)} %tok_in.1, bf16[128,1024]{1,0:T(8,128)(2,1)} %og_in.1, f32[8,128]{1,0:T(8,128)} %maximum_maximum_fusion.meta_in, bf16[224,1024]{1,0:T(8,128)(2,1)} %wg.1, ...), custom_call_target="tpu_custom_call" | custom-call | tf_op jit(solution)/shard_map/pallas_call | solution.py:383
  126.4 0.0 copy-start.2
  126.4 1.7 %copy.18 = bf16[128,1024]{1,0:T(8,128)(2,1)} copy(bf16[128,1024]{1,0:T(8,128)(2,1)} %get-tuple-element.8) | data formatting | bytes 524288
  128.2 0.0 copy-done.2
  128.2 0.0 copy-start.1
  128.2 0.8 copy.19
  128.9 0.4 copy-done.1
  129.4 0.0 copy-start
  129.4 0.8 copy.20
  130.1 0.4 copy-done
  130.5 0.8 copy.21
  (6 shorter events, 0.1 us)
Async XLA Ops:
  0.6 0.7 copy-start.3
  2.9 0.7 copy-start.4
  126.4 1.7 %copy-start.2 = (bf16[224,1024]{1,0:T(8,128)(2,1)S(1)}, bf16[224,1024]{1,0:T(8,128)(2,1)}, u32[]{:S(2)}) copy-start(bf16[224,1024]{1,0:T(8,128)(2,1)} %get-tuple-element.9) | copy-start | bytes 1376260
  128.2 1.2 copy-start.1
  129.4 1.2 copy-start

commit v2 on v1

v2 whole, which is shorter than its diff:
```python
import jax
import jax.numpy as jnp
from jax import lax
from jax.experimental import pallas as pl
from jax.experimental.pallas import tpu as pltpu
from jax.sharding import PartitionSpec as P

NX, NY, NZ = 4, 4, 8
SLICES = 8
SLOT = 40
CODE = 64
TOK = 128
PER_Y = NZ * SLOT
ROWS = NY * PER_Y
GROUP = 64
CHUNK = NY * GROUP
NCH = PER_Y // GROUP
WINDOW = 48
TILE = 256
STEP, EARLY = 80, 48
BACK = ((272, 48), (192, 80), (112, 80), (32, 80), (0, 32))
PLACE = (0, 1, 3, 5, 7, 6, 4, 2)
MESH = pl.DeviceIdType.MESH
BF = jnp.bfloat16
F32 = jnp.float32
CROSS_LAST = (((1,), (1,)), ((), ()))
CROSS_FIRST = (((0,), (0,)), ((), ()))
PLAIN = (((1,), (0,)), ((), ()))


def dot(a, b, dims):
    return lax.dot_general(a, b, dims, preferred_element_type=F32)


def layer_kernel(
    tok_in, og_in, ids, route, wg, wu, wd,
    out, g_gate, g_up, g_down,
    w, meta, src_rows, xc, staged, hit_s, scale_s,
    part, part_in, mid, hid, part_h, part_h_in, mid_h, grads_x,
    up_s, act_s, slope_s, rows_out, rows_back,
    back_w, sum_s, ring_out, ring_in, acc, pair_out, pair_in,
    w_loc, w_send, w_recv, m_send, m_recv, own_sem,
    z_send, z_recv, y_send, y_recv,
    pm_send, pm_recv, p_send, p_recv, h_send, h_recv, h2_send, h2_recv,
    hm_send, hm_recv, ph_send, ph_recv, gx_send, gx_recv, g2_send, g2_recv,
    o_send, o_recv, r_send, r_recv, pair_send, pair_recv,
):
    own_h, feats = wg.shape
    half_f = feats // 2
    chip_h = 2 * own_h
    quarter_h = chip_h // NX
    x = lax.axis_index("dp")
    e = lax.axis_index("expert")
    c = lax.rem(e, 2)
    chip = e // 2
    z = lax.rem(chip, NZ)
    y = chip // NZ
    half = z // 4
    sibling = e + 1 - 2 * c

    def chip_at(dy, dz):
        return (x, (lax.rem(y + dy, NY) * NZ + lax.rem(z + dz, NZ)) * 2 + c)

    def x_peer(k):
        return lax.rem(x + k, NX)

    def remote(src, dst, send_sem, recv_sem, dev):
        return pltpu.make_async_remote_copy(
            src_ref=src, dst_ref=dst, send_sem=send_sem, recv_sem=recv_sem,
            device_id=dev, device_id_type=MESH)

    def wait_bytes(ref, sem):
        pltpu.make_async_copy(ref, ref, sem).wait()

    def set_meta():
        slices = lax.div(ids[...], 8)
        number = lax.broadcasted_iota(jnp.int32, (SLICES, TOK), 0)
        hit0 = (slices[0:1] == number).astype(F32)
        hit1 = (slices[1:2] == number).astype(F32)
        earlier = (lax.broadcasted_iota(jnp.int32, (TOK, TOK), 0)
                   < lax.broadcasted_iota(jnp.int32, (TOK, TOK), 1)).astype(F32).astype(BF)
        before = dot((hit0 + hit1).astype(BF), earlier, PLAIN)
        code = slices.astype(F32) * float(CODE)
        meta[0, 0:1] = code[0:1] + jnp.sum(hit0 * before, axis=0, keepdims=True)
        meta[0, 1:2] = code[1:2] + jnp.sum(hit1 * (before + hit0), axis=0, keepdims=True)
        meta[0, 2:4] = route[...]
        meta[0, 4:8] = jnp.zeros((4, TOK), F32)
        meta[NZ] = jnp.full((8, TOK), -1.0, F32)

    def each(count, f):
        lax.fori_loop(0, count, lambda i, carry: (f(i), carry)[1], 0)

    def blank(row):
        for a in range(2):
            src_rows[a, NZ, pl.ds(pl.multiple_of(row * 16, 16), 16)] = jnp.zeros((16, feats), BF)
            ring_in[a, 0, pl.ds(pl.multiple_of(row * 16, 16), 16), (1 - a) * half_f:(2 - a) * half_f] = (
                jnp.zeros((16, half_f), BF))

    def clear(row):
        for kind in range(3):
            acc[kind, pl.ds(pl.multiple_of(row * 16, 16), 16)] = jnp.zeros((16, feats), F32)

    def weights(dy, place, first, count):
        codes = meta[place, 0:2, :] - ((lax.rem(y + dy, NY) * 2 + half) * CODE).astype(F32)
        start = jnp.asarray(place * SLOT, jnp.int32).astype(F32)
        at = jnp.where((codes >= 0.0) & (codes < float(SLOT)), codes + start, -1.0)
        row = (lax.broadcasted_iota(jnp.int32, (count, TOK), 0) + first).astype(F32)
        return (jnp.where(row == at[0:1], meta[place, 2:3, :], 0.0)
                + jnp.where(row == at[1:2], meta[place, 3:4, :], 0.0))

    def spans(first, count):
        found, row = [], first
        while row < first + count:
            i = row // GROUP
            n = min(first + count, (i + 1) * GROUP) - row
            found.append((i, row - i * GROUP, row, n))
            row += n
        return found

    def choose(a, first, count, place, places):
        def one_y(dy):
            wts = jnp.concatenate([weights(dy, place + n, first, count) for n in range(places)], axis=1)
            here = pl.ds(pl.multiple_of(dy * count, 16), count)
            hit_s[here, 0:places * TOK] = (wts > 0.0).astype(F32).astype(BF)
            total = jnp.sum(wts, axis=1, keepdims=True)
            scale_s[here] = jnp.broadcast_to(jnp.where(a == 1, total, jnp.ones_like(total)), (count, TOK))

        def tile(n):
            lanes = pl.ds(pl.multiple_of(n * TILE, TILE), TILE)
            rows = src_rows[a, pl.ds(place, places), :, lanes].reshape(places * TOK, TILE)
            picked = dot(hit_s[0:NY * count, 0:places * TOK], rows, PLAIN)
            picked = (scale_s[0:NY * count, 0:1] * picked).astype(BF)
            for dy in range(NY):
                staged[a, dy, pl.ds(pl.multiple_of(first, 16), count), lanes] = picked[dy * count:(dy + 1) * count]

        each(NY, one_y)
        each(feats // TILE, tile)

    barrier = pltpu.get_barrier_semaphore()
    friends = [chip_at(0, d) for d in range(1, NZ)] + [chip_at(d, 0) for d in range(1, NY)]
    friends += [(x_peer(k), e) for k in range(1, NX)] + [(x, sibling)]
    for dev in friends:
        pl.semaphore_signal(barrier, inc=1, device_id=dev, device_id_type=MESH)
    pltpu.make_async_copy(tok_in, src_rows.at[0, 0], own_sem.at[0]).start()
    pltpu.make_async_copy(og_in, src_rows.at[1, 0], own_sem.at[1]).start()
    set_meta()
    for a in range(2):
        wait_bytes(src_rows.at[a, 0], own_sem.at[a])
    each(2, lambda a: choose(a, 0, 32, 0, 1))
    pl.semaphore_wait(barrier, len(friends))

    def ring_send(a, k, own=None):
        for d in range(2):
            if k == 1:
                src, dst = own, src_rows.at[a, 1 + d]
            else:
                src, dst = src_rows.at[a, 2 * k - 3 + d], src_rows.at[a, 2 * k - 1 + d if k < 4 else 7]
            if k == 4:
                lanes = pl.ds(d * half_f, half_f)
                src, dst = src.at[:, lanes], dst.at[:, lanes]
            remote(src, dst, z_send.at[a, d, k - 1], z_recv.at[a, d, k - 1],
                   chip_at(0, 1 if d == 0 else NZ - 1)).start()

    def ring_wait(a, k):
        for d in range(2):
            ref = src_rows.at[a, 2 * k - 1 + d] if k < 4 else src_rows.at[a, 7, :, pl.ds(d * half_f, half_f)]
            wait_bytes(ref, z_recv.at[a, d, k - 1])

    ring_send(0, 1, tok_in)
    for d in range(1, NZ):
        remote(meta.at[0], meta.at[PLACE[d]], m_send, m_recv, chip_at(0, d)).start()

    def w_part(i, core):
        return w.at[i, pl.ds(pl.multiple_of(core * own_h, 16), own_h)]

    def pass_on(a, first, count):
        for dy in (1, 3, 2):
            for i, off, row, n in spans(first, count):
                remote(staged.at[a, dy, pl.ds(row, n)], xc.at[a, i, dy, pl.ds(off, n)],
                       y_send.at[a, dy - 1], y_recv.at[a, i], chip_at(dy, 0)).start()
        for i, off, row, n in spans(first, count):
            pltpu.make_async_copy(staged.at[a, 0, pl.ds(row, n)], xc.at[a, i, 0, pl.ds(off, n)],
                                  y_recv.at[a, i]).start()

    def relay_step(a, k):
        for j in range(1, 5):
            @pl.when(k == j)
            def _(j=j):
                ring_wait(a, j)
                if j < 4:
                    ring_send(a, j + 1)
        choose(a, STEP * k - EARLY, STEP, 2 * k - 2, 3)
        for j in range(1, 5):
            @pl.when(k == j)
            def _(j=j):
                pass_on(a, STEP * j - EARLY, min(STEP, PER_Y - STEP * j + EARLY))

    left, far, right = x_peer(NX - 1), x_peer(2), x_peer(1)
    near_half, far_half = pl.ds(0, CHUNK // 2), pl.ds(CHUNK // 2, CHUNK // 2)

    def both_sides(rightward, leftward, send, recv, i):
        for d, (src, dst) in enumerate((rightward, leftward)):
            remote(src, dst, send.at[d, i], recv.at[d, i], ((right, left)[d], e)).start()

    def add_to(ref, extra):
        ref[...] = (ref[...].astype(F32) + extra.astype(F32)).astype(BF)

    def chunk(ref, i):
        return xc[ref, i].reshape(CHUNK, feats)

    def up_gate(i):
        rows = chunk(0, i)

        def one(kind):
            prod = dot(w[kind], rows, CROSS_LAST).astype(BF)
            for q in range(NX):
                part[q, i, kind] = prod[q * quarter_h:(q + 1) * quarter_h]

        each(2, one)
        both_sides((part.at[far, i, 0], mid.at[0, i]), (part.at[far, i, 1], mid.at[1, i]), pm_send, pm_recv, i)

    def up_gate_mid(i):
        wait_bytes(mid.at[0, i], pm_recv.at[0, i])
        wait_bytes(mid.at[1, i], pm_recv.at[1, i])
        add_to(part.at[right, i, 0], mid[0, i])
        add_to(part.at[left, i, 1], mid[1, i])
        both_sides((part.at[right, i], part_in.at[0, i]), (part.at[left, i], part_in.at[1, i]), p_send, p_recv, i)

    def act(i):
        for d in range(2):
            wait_bytes(part_in.at[d, i], p_recv.at[d, i])
        gate = part[x, i, 0].astype(F32)
        up = part[x, i, 1].astype(F32)
        for d in range(2):
            gate += part_in[d, i, 0].astype(F32)
            up += part_in[d, i, 1].astype(F32)
        sig = jax.nn.sigmoid(gate)
        active = gate * sig
        up_s[i] = up
        act_s[i] = active
        slope_s[i] = sig * (1.0 + gate * (1.0 - sig))
        hid[i, x] = (active * up).astype(BF)
        both_sides((hid.at[i, x], hid.at[i, x]), (hid.at[i, x], hid.at[i, x]), h_send, h_recv, i)

    def hid_pass(i):
        wait_bytes(hid.at[i, left], h_recv.at[0, i])
        wait_bytes(hid.at[i, right], h_recv.at[1, i])
        both_sides((hid.at[i, left, :, near_half],) * 2, (hid.at[i, right, :, far_half],) * 2, h2_send, h2_recv, i)

    def expert_out(i):
        wait_bytes(hid.at[i, far, :, near_half], h2_recv.at[0, i])
        wait_bytes(hid.at[i, far, :, far_half], h2_recv.at[1, i])
        prod = dot(hid[i].reshape(chip_h, CHUNK), w[2], CROSS_FIRST).astype(BF)
        rows_back[0, pl.ds(pl.multiple_of(i * GROUP, GROUP), GROUP)] = prod[0:GROUP]
        for dy in range(1, NY):
            rows_out[i, dy - 1] = prod[dy * GROUP:(dy + 1) * GROUP]

    def hidden_part(i):
        prod = dot(w[2], chunk(1, i), CROSS_LAST).astype(BF)
        for q in range(NX):
            part_h[q, i] = prod[q * quarter_h:(q + 1) * quarter_h]
        both_sides((part_h.at[far, i, :, near_half], mid_h.at[0, i]),
                   (part_h.at[far, i, :, far_half], mid_h.at[1, i]), hm_send, hm_recv, i)

    def hidden_mid(i):
        wait_bytes(mid_h.at[0, i], hm_recv.at[0, i])
        wait_bytes(mid_h.at[1, i], hm_recv.at[1, i])
        add_to(part_h.at[right, i, :, near_half], mid_h[0, i])
        add_to(part_h.at[left, i, :, far_half], mid_h[1, i])
        both_sides((part_h.at[right, i], part_h_in.at[0, i]), (part_h.at[left, i], part_h_in.at[1, i]),
                   ph_send, ph_recv, i)

    def grad_rows(i):
        for d in range(2):
            wait_bytes(part_h_in.at[d, i], ph_recv.at[d, i])
        gh = part_h[x, i].astype(F32)
        for d in range(2):
            gh += part_h_in[d, i].astype(F32)
        grads_x[i, x, 0] = (gh * up_s[i] * slope_s[i]).astype(BF)
        grads_x[i, x, 1] = (gh * act_s[i]).astype(BF)
        both_sides((grads_x.at[i, x],) * 2, (grads_x.at[i, x],) * 2, gx_send, gx_recv, i)

    def grads_pass(i):
        wait_bytes(grads_x.at[i, left], gx_recv.at[0, i])
        wait_bytes(grads_x.at[i, right], gx_recv.at[1, i])
        both_sides((grads_x.at[i, left, 0],) * 2, (grads_x.at[i, right, 1],) * 2, g2_send, g2_recv, i)

    def down_step(i):
        acc[2] += dot(hid[i].reshape(chip_h, CHUNK), chunk(1, i), PLAIN)

    def gate_step(i):
        wait_bytes(grads_x.at[i, far, 0], g2_recv.at[0, i])
        wait_bytes(grads_x.at[i, far, 1], g2_recv.at[1, i])

        def one(kind):
            acc[kind] += dot(grads_x[i, :, kind].reshape(chip_h, CHUNK), chunk(0, i), PLAIN)

        each(2, one)

    def give_back(first, count, g):
        for dy in (1, 3, 2):
            for i, off, row, n in spans(first, count):
                remote(rows_out.at[i, dy - 1, pl.ds(off, n)], rows_back.at[dy, pl.ds(row, n)],
                       o_send.at[g], o_recv.at[g], chip_at(NY - dy, 0)).start()

    def await_back(g):
        first, count = BACK[g]
        wait_bytes(rows_back.at[pl.ds(1, NY - 1), pl.ds(first, count)], o_recv.at[g])

    def dense(place):
        first = pl.multiple_of(place * SLOT // 16 * 16, 16)

        def one_y(dy):
            wts = weights(dy, place, first, WINDOW)
            coarse = wts.astype(BF)
            here = pl.ds(pl.multiple_of(dy * WINDOW, 16), WINDOW)
            back_w[0, here] = coarse
            back_w[1, here] = (wts - coarse.astype(F32)).astype(BF)

        def tile(n):
            lanes = pl.ds(pl.multiple_of(n * TILE, TILE), TILE)
            rows = rows_back[:, pl.ds(first, WINDOW), lanes].reshape(NY * WINDOW, TILE)
            sum_s[:, lanes] = dot(back_w[0], rows, CROSS_FIRST) + dot(back_w[1], rows, CROSS_FIRST)

        each(NY, one_y)
        each(feats // TILE, tile)

    def fold_send(k, d):
        src, dst = ring_out.at[d, k - 1], ring_in.at[d, k - 1]
        if k == 1:
            lanes = pl.ds(d * half_f, half_f)
            src, dst = src.at[:, lanes], dst.at[:, lanes]
        remote(src, dst, r_send.at[d, k - 1], r_recv.at[d, k - 1], chip_at(0, 1 if d == 0 else NZ - 1)).start()

    def fold_wait(k, d):
        ref = ring_in.at[d, k - 1]
        wait_bytes(ref.at[:, pl.ds(d * half_f, half_f)] if k == 1 else ref, r_recv.at[d, k - 1])

    def fold(n):
        for j, groups in ((0, (0,)), (1, (1,)), (3, (2,)), (5, (3,)), (7, (4,))):
            @pl.when(n == j)
            def _(groups=groups):
                for g in groups:
                    await_back(g)
        dense(7 - n)

        @pl.when(n == 0)
        def _():
            for d in range(2):
                ring_out[d, 0] = sum_s[...].astype(BF)
                fold_send(1, d)

        for j in range(1, 7):
            @pl.when(n == j)
            def _(k=(j + 3) // 2, d=(j - 1) % 2):
                fold_wait(k - 1, d)

        @pl.when((n >= 1) & (n <= 6))
        def _():
            k = (n + 3) // 2
            d = lax.rem(n - 1, 2)
            ring_out[d, k - 1] = (sum_s[...] + ring_in[d, k - 2].astype(F32)).astype(BF)

        for j in range(1, 7):
            @pl.when(n == j)
            def _(k=(j + 3) // 2, d=(j - 1) % 2):
                fold_send(k, d)

    def send_pair(kind):
        pair_out[kind] = acc[kind, pl.ds(pl.multiple_of((1 - c) * own_h, 16), own_h)].astype(BF)
        remote(pair_out.at[kind], pair_in.at[kind], pair_send.at[kind], pair_recv.at[kind],
               (x, sibling)).start()

    def join_pair(kind, dest):
        wait_bytes(pair_in.at[kind], pair_recv.at[kind])
        dest[...] = (acc[kind, pl.ds(pl.multiple_of(c * own_h, 16), own_h)]
                     + pair_in[kind].astype(F32)).astype(BF)

    def tok_chunk(i):
        wait_bytes(xc.at[0, i], y_recv.at[0, i])
        up_gate(i)

    def cot_chunk(i):
        wait_bytes(xc.at[1, i], y_recv.at[1, i])
        hidden_part(i)

    def weights_here():
        for i, src in enumerate((wg, wu, wd)):
            wait_bytes(w_part(i, c), w_loc.at[i])
            wait_bytes(w_part(i, 1 - c), w_recv.at[i])

    for a in range(2):
        pass_on(a, 0, 32)
    for i, src in enumerate((wg, wu, wd)):
        remote(src, w_part(i, c), w_send.at[i], w_recv.at[i], (x, sibling)).start()
        pltpu.make_async_copy(src, w_part(i, c), w_loc.at[i]).start()
    each(TOK // 16, blank)
    wait_bytes(meta.at[pl.ds(1, NZ - 1)], m_recv)
    each(chip_h // 16, clear)
    weights_here()

    def during(lo, t, f):
        @pl.when((t >= lo) & (t < lo + NCH))
        def _():
            f(t - lo)

    def step(t):
        @pl.when(t < 8)
        def _():
            relay_step(t // 4, lax.rem(t, 4) + 1)

        @pl.when(t == 2)
        def _():
            ring_send(1, 1, og_in)

        during(1, t, tok_chunk)
        during(2, t, up_gate_mid)
        during(3, t, act)
        during(4, t, hid_pass)
        during(5, t, expert_out)

        @pl.when(t == 9)
        def _():
            for g, rows in enumerate(BACK):
                give_back(*rows, g)

        during(8, t, cot_chunk)
        during(9, t, hidden_mid)
        during(10, t, grad_rows)
        during(9, t, down_step)
        during(11, t, grads_pass)
        during(12, t, gate_step)

        @pl.when(t == 13)
        def _():
            send_pair(2)

        @pl.when(t == 16)
        def _():
            send_pair(0)
            send_pair(1)

        def from_step(start, n):
            return jnp.where(t >= start, n, 0)

        done = from_step(14, 1) + from_step(16, 2) + from_step(18, 2) + from_step(20, 2)
        due = from_step(13, 1) + from_step(15, 2) + from_step(17, 2) + from_step(19, 2) + from_step(20, 1)
        lax.fori_loop(done, due, lambda n, carry: (fold(n), carry)[1], 0)

        @pl.when(t == 18)
        def _():
            join_pair(2, g_down)
            join_pair(0, g_gate)
            join_pair(1, g_up)

    each(21, step)
    mine = sum_s[...]

    for d in range(2):
        fold_wait(4, d)
        mine += ring_in[d, 3].astype(F32)
    out[...] = mine.astype(BF)

    for i in range(3):
        wait_bytes(wg, w_send.at[i])
        wait_bytes(pair_out.at[i], pair_send.at[i])
    wait_bytes(meta.at[pl.ds(1, NZ - 1)], m_send)
    for d in range(2):
        lanes = pl.ds(d * half_f, half_f)
        for k in range(1, 5):
            for a in range(2):
                wait_bytes(src_rows.at[a, 0] if k < 4 else src_rows.at[a, 0, :, lanes], z_send.at[a, d, k - 1])
            wait_bytes(ring_out.at[d, k - 1] if k > 1 else ring_out.at[d, 0, :, lanes], r_send.at[d, k - 1])
    for dy in range(1, NY):
        for a in range(2):
            wait_bytes(staged.at[a, dy, pl.ds(0, PER_Y)], y_send.at[a, dy - 1])
    for g, (first, count) in enumerate(BACK):
        wait_bytes(rows_back.at[pl.ds(1, NY - 1), pl.ds(0, count)], o_send.at[g])
    for i in range(NCH):
        for d in range(2):
            wait_bytes(mid.at[d, i], pm_send.at[d, i])
            wait_bytes(part_in.at[d, i], p_send.at[d, i])
            wait_bytes(hid.at[i, x], h_send.at[d, i])
            wait_bytes(mid_h.at[d, i], h2_send.at[d, i])
            wait_bytes(mid_h.at[d, i], hm_send.at[d, i])
            wait_bytes(part_h_in.at[d, i], ph_send.at[d, i])
            wait_bytes(grads_x.at[i, x], gx_send.at[d, i])
            wait_bytes(grads_x.at[i, x, 0], g2_send.at[d, i])


def finish_kernel(*refs):
    count = (len(refs) - 2) // 3
    results, outs, held = refs[:count], refs[count:2 * count], refs[2 * count:3 * count]
    sem_in, sem_out = refs[-2:]
    first = [pltpu.make_async_copy(results[i], held[i], sem_in.at[i]) for i in range(count)]
    last = [pltpu.make_async_copy(held[i], outs[i], sem_out.at[i]) for i in range(count)]
    for copy in first:
        copy.start()
    for i in range(count):
        first[i].wait()
        last[i].start()
    for copy in last:
        copy.wait()


def finish(results):
    anywhere = pl.BlockSpec(memory_space=pl.ANY)
    count = len(results)
    return pl.pallas_call(
        finish_kernel,
        out_shape=tuple(jax.ShapeDtypeStruct(r.shape, r.dtype) for r in results),
        in_specs=[anywhere] * count,
        out_specs=[anywhere] * count,
        scratch_shapes=[pltpu.VMEM(r.shape, r.dtype) for r in results]
        + [pltpu.SemaphoreType.DMA((count,)), pltpu.SemaphoreType.DMA((count,))],
    )(*results)


def run_layer(tokens, out_grad, ids, route, wg, wu, wd):
    own_h, feats = wg.shape
    qh = 2 * own_h // NX
    dma = pltpu.SemaphoreType.DMA
    vm = pltpu.VMEM
    scratch = [
        vm((3, 2 * own_h, feats), BF), vm((NZ + 1, 8, TOK), F32),
        vm((2, NZ + 1, TOK, feats), BF), vm((2, NCH, NY, GROUP, feats), BF),
        vm((2, NY, 4 * STEP - EARLY + STEP, feats), BF),
        vm((NY * STEP, 3 * TOK), BF), vm((NY * STEP, TOK), F32),
        vm((NX, NCH, 2, qh, CHUNK), BF), vm((2, NCH, 2, qh, CHUNK), BF), vm((2, NCH, qh, CHUNK), BF),
        vm((NCH, NX, qh, CHUNK), BF),
        vm((NX, NCH, qh, CHUNK), BF), vm((2, NCH, qh, CHUNK), BF), vm((2, NCH, qh, CHUNK // 2), BF),
        vm((NCH, NX, 2, qh, CHUNK), BF),
        vm((NCH, qh, CHUNK), F32), vm((NCH, qh, CHUNK), F32), vm((NCH, qh, CHUNK), F32),
        vm((NCH, NY - 1, GROUP, feats), BF), vm((NY, PER_Y, feats), BF),
        vm((2, NY * WINDOW, TOK), BF), vm((TOK, feats), F32),
        vm((2, 4, TOK, feats), BF), vm((2, 4, TOK, feats), BF),
        vm((3, 2 * own_h, feats), F32),
        vm((3, own_h, feats), BF), vm((3, own_h, feats), BF),
        dma((3,)), dma((3,)), dma((3,)), dma, dma, dma((2,)),
        dma((2, 2, 4)), dma((2, 2, 4)), dma((2, NY - 1)), dma((2, NCH)),
        *[dma((2, NCH))] * 16,
        dma((len(BACK),)), dma((len(BACK),)), dma((2, 4)), dma((2, 4)),
        dma((3,)), dma((3,)),
    ]
    anywhere = pl.BlockSpec(memory_space=pl.ANY)
    inside = pl.BlockSpec(memory_space=pltpu.VMEM)
    return pl.pallas_call(
        layer_kernel,
        out_shape=(
            jax.ShapeDtypeStruct((TOK, feats), BF),
            jax.ShapeDtypeStruct((own_h, feats), BF),
            jax.ShapeDtypeStruct((own_h, feats), BF),
            jax.ShapeDtypeStruct((own_h, feats), BF),
        ),
        in_specs=[anywhere] * 2 + [inside] * 2 + [anywhere] * 3,
        out_specs=[inside] * 4,
        scratch_shapes=scratch,
        compiler_params=pltpu.CompilerParams(
            collective_id=0, has_side_effects=True, vmem_limit_bytes=60 * 1024 * 1024),
    )(tokens, out_grad, ids, route, wg, wu, wd)


def per_device(tokens, expert_ids, route_weights, w_gate, w_up, w_down, out_grad):
    return finish(run_layer(
        tokens, out_grad, expert_ids.T, route_weights.T, w_gate, w_up, w_down))


def solution(mesh):
    placed = (
        P("expert", "dp"),
        P("expert", None),
        P("expert", None),
        P("expert", "dp"),
        P("expert", "dp"),
        P("expert", "dp"),
        P("expert", "dp"),
    )
    return jax.shard_map(
        per_device,
        mesh=mesh,
        in_specs=placed,
        out_specs=(P("expert", "dp"), P("expert", "dp"), P("expert", "dp"), P("expert", "dp")),
        check_vma=False,
    )
```

time: 133 us -> 129 us (0.970)
  local copies, waits for them, and re-layouts: 7.01 us -> 0 us
  Pallas kernels: 122 us -> 128 us
  other arithmetic: 1.42 us -> 0 us
    unnamed x14 -> x0, local copies, waits for them, and re-layouts: 6.13 us -> none
    pallas_call x1, Pallas kernels: 122 us -> 125 us  [run_layer(): pl.pallas_call(layer_kernel, out_shape=(jax.ShapeDtypeStruct((TOK, feats)...]
    pallas_call x0 -> x1, Pallas kernels: none -> 2.24 us  [finish(): pl.pallas_call(finish_kernel, out_shape=tuple((jax.ShapeDtypeStruct(r.sha...]
where the time goes in v2:
time: 129 us; the launch traced here: 128 us
  Pallas kernels  128 us (99%)
    pallas_call x1, Pallas kernels, run_layer(): pl.pallas_call(layer_kernel, out_shape=(jax.ShapeDtypeStruct((TOK, feats)...  125 us

profile of v2, /device:TPU:64, one launch (start us, length us, event | category | flops | bytes accessed | tf_op | source)
XLA Modules:
  0.0 128.3 jit_solution(7820050333079536606)
XLA Ops:
  0.6 125.4 %shard_map.102 = (bf16[128,1024]{1,0:T(8,128)(2,1)}, bf16[224,1024]{1,0:T(8,128)(2,1)}, bf16[224,1024]{1,0:T(8,128)(2,1)}, bf16[224,1024]{1,0:T(8,128)(2,1)}) custom-call(bf16[128,1024]{1,0:T(8,128)(2,1)} %tok_in.1, bf16[128,1024]{1,0:T(8,128)(2,1)} %og_in.1, s32[2,128]{1,0:T(2,128)} %bitcast.2, f32[2,128]{1,0:T(2,128)} %bitcast.3, bf16[224,1024]{1,0:T(8,128)(2,1)} %wg.1, ...), custom_call_target="tpu_custom_call" | custom-call | tf_op jit(solution)/shard_map/pallas_call | solution.py:547
  126.1 2.2 %shard_map.103 = (bf16[128,1024]{1,0:T(8,128)(2,1)}, bf16[224,1024]{1,0:T(8,128)(2,1)}, bf16[224,1024]{1,0:T(8,128)(2,1)}, bf16[224,1024]{1,0:T(8,128)(2,1)}) custom-call(bf16[128,1024]{1,0:T(8,128)(2,1)} %get-tuple-element.8.refs_0_, bf16[224,1024]{1,0:T(8,128)(2,1)} %get-tuple-element.9.refs_1_, bf16[224,1024]{1,0:T(8,128)(2,1)} %get-tuple-element.10.refs_2_, ...), custom_call_target="tpu_custom_call" | custom-call | tf_op jit(solution)/shard_map/pallas_call | solution.py:509

commit v3 on v2

--- a/solution.py
+++ b/solution.py
@@ -424,18 +424,18 @@
             for g, rows in enumerate(BACK):
                 give_back(*rows, g)
 
-        during(8, t, cot_chunk)
-        during(9, t, hidden_mid)
-        during(10, t, grad_rows)
+        during(7, t, cot_chunk)
+        during(8, t, hidden_mid)
+        during(9, t, grad_rows)
         during(9, t, down_step)
-        during(11, t, grads_pass)
-        during(12, t, gate_step)
+        during(10, t, grads_pass)
+        during(11, t, gate_step)
 
         @pl.when(t == 13)
         def _():
             send_pair(2)
 
-        @pl.when(t == 16)
+        @pl.when(t == 15)
         def _():
             send_pair(0)
             send_pair(1)
@@ -443,17 +443,17 @@
         def from_step(start, n):
             return jnp.where(t >= start, n, 0)
 
-        done = from_step(14, 1) + from_step(16, 2) + from_step(18, 2) + from_step(20, 2)
-        due = from_step(13, 1) + from_step(15, 2) + from_step(17, 2) + from_step(19, 2) + from_step(20, 1)
+        done = from_step(11, 1) + from_step(12, 2) + from_step(14, 2) + from_step(15, 2) + from_step(17, 1)
+        due = from_step(10, 1) + from_step(11, 2) + from_step(13, 2) + from_step(14, 2) + from_step(16, 1)
         lax.fori_loop(done, due, lambda n, carry: (fold(n), carry)[1], 0)
 
-        @pl.when(t == 18)
+        @pl.when(t == 16)
         def _():
             join_pair(2, g_down)
             join_pair(0, g_gate)
             join_pair(1, g_up)
 
-    each(21, step)
+    each(17, step)
     mine = sum_s[...]
 
     for d in range(2):

time: 129 us -> 119 us (0.922)
  Pallas kernels: 128 us -> 119 us
    pallas_call x1, Pallas kernels: 125 us -> 116 us  [run_layer(): pl.pallas_call(layer_kernel, out_shape=(jax.ShapeDtypeStruct((TOK, feats)...]
where the time goes in v3:
time: 119 us
  Pallas kernels  119 us (100%)
    pallas_call x1, Pallas kernels, run_layer(): pl.pallas_call(layer_kernel, out_shape=(jax.ShapeDtypeStruct((TOK, feats)...  116 us

profile of v3, /device:TPU:64, one launch (start us, length us, event | category | flops | bytes accessed | tf_op | source)
XLA Modules:
  0.0 119.2 jit_solution(14521187952988792371)
XLA Ops:
  0.6 116.3 %shard_map.102 = (bf16[128,1024]{1,0:T(8,128)(2,1)}, bf16[224,1024]{1,0:T(8,128)(2,1)}, bf16[224,1024]{1,0:T(8,128)(2,1)}, bf16[224,1024]{1,0:T(8,128)(2,1)}) custom-call(bf16[128,1024]{1,0:T(8,128)(2,1)} %tok_in.1, bf16[128,1024]{1,0:T(8,128)(2,1)} %og_in.1, s32[2,128]{1,0:T(2,128)} %bitcast.2, f32[2,128]{1,0:T(2,128)} %bitcast.3, bf16[224,1024]{1,0:T(8,128)(2,1)} %wg.1, ...), custom_call_target="tpu_custom_call" | custom-call | tf_op jit(solution)/shard_map/pallas_call | solution.py:547
  117.0 2.2 %shard_map.103 = (bf16[128,1024]{1,0:T(8,128)(2,1)}, bf16[224,1024]{1,0:T(8,128)(2,1)}, bf16[224,1024]{1,0:T(8,128)(2,1)}, bf16[224,1024]{1,0:T(8,128)(2,1)}) custom-call(bf16[128,1024]{1,0:T(8,128)(2,1)} %get-tuple-element.8.refs_0_, bf16[224,1024]{1,0:T(8,128)(2,1)} %get-tuple-element.9.refs_1_, bf16[224,1024]{1,0:T(8,128)(2,1)} %get-tuple-element.10.refs_2_, ...), custom_call_target="tpu_custom_call" | custom-call | tf_op jit(solution)/shard_map/pallas_call | solution.py:509

commit v4 on v3

--- a/solution.py
+++ b/solution.py
@@ -373,8 +373,9 @@
 
     def join_pair(kind, dest):
         wait_bytes(pair_in.at[kind], pair_recv.at[kind])
-        dest[...] = (acc[kind, pl.ds(pl.multiple_of(c * own_h, 16), own_h)]
-                     + pair_in[kind].astype(F32)).astype(BF)
+        pair_in[kind] = (acc[kind, pl.ds(pl.multiple_of(c * own_h, 16), own_h)]
+                         + pair_in[kind].astype(F32)).astype(BF)
+        pltpu.make_async_copy(pair_in.at[kind], dest, w_loc.at[kind]).start()
 
     def tok_chunk(i):
         wait_bytes(xc.at[0, i], y_recv.at[0, i])
@@ -463,6 +464,7 @@
 
     for i in range(3):
         wait_bytes(wg, w_send.at[i])
+        wait_bytes(pair_in.at[i], w_loc.at[i])
         wait_bytes(pair_out.at[i], pair_send.at[i])
     wait_bytes(meta.at[pl.ds(1, NZ - 1)], m_send)
     for d in range(2):
@@ -553,7 +555,7 @@
             jax.ShapeDtypeStruct((own_h, feats), BF),
         ),
         in_specs=[anywhere] * 2 + [inside] * 2 + [anywhere] * 3,
-        out_specs=[inside] * 4,
+        out_specs=[inside] + [anywhere] * 3,
         scratch_shapes=scratch,
         compiler_params=pltpu.CompilerParams(
             collective_id=0, has_side_effects=True, vmem_limit_bytes=60 * 1024 * 1024),

time: 119 us -> 119 us (level)
  no operation moved by 1% of the time
where the time goes in v4:
time: 119 us
  Pallas kernels  118 us (99%)
    pallas_call x1, Pallas kernels, run_layer(): pl.pallas_call(layer_kernel, out_shape=(jax.ShapeDtypeStruct((TOK, feats)...  116 us

profile of v4, /device:TPU:64, one launch (start us, length us, event | category | flops | bytes accessed | tf_op | source)
XLA Modules:
  0.0 118.8 jit_solution(3887118814907943635)
XLA Ops:
  0.6 115.9 %shard_map.102 = (bf16[128,1024]{1,0:T(8,128)(2,1)}, bf16[224,1024]{1,0:T(8,128)(2,1)}, bf16[224,1024]{1,0:T(8,128)(2,1)}, bf16[224,1024]{1,0:T(8,128)(2,1)}) custom-call(bf16[128,1024]{1,0:T(8,128)(2,1)} %tok_in.1, bf16[128,1024]{1,0:T(8,128)(2,1)} %og_in.1, s32[2,128]{1,0:T(2,128)} %bitcast.2, f32[2,128]{1,0:T(2,128)} %bitcast.3, bf16[224,1024]{1,0:T(8,128)(2,1)} %wg.1, ...), custom_call_target="tpu_custom_call" | custom-call | tf_op jit(solution)/shard_map/pallas_call | solution.py:549
  116.6 2.2 %shard_map.103 = (bf16[128,1024]{1,0:T(8,128)(2,1)}, bf16[224,1024]{1,0:T(8,128)(2,1)}, bf16[224,1024]{1,0:T(8,128)(2,1)}, bf16[224,1024]{1,0:T(8,128)(2,1)}) custom-call(bf16[128,1024]{1,0:T(8,128)(2,1)} %get-tuple-element.8.refs_0_, bf16[224,1024]{1,0:T(8,128)(2,1)} %get-tuple-element.9.refs_1_, bf16[224,1024]{1,0:T(8,128)(2,1)} %get-tuple-element.10.refs_2_, ...), custom_call_target="tpu_custom_call" | custom-call | tf_op jit(solution)/shard_map/pallas_call | solution.py:511
